TPU v7x, 32 devices: a whole 2x2x4 slice. The times are simulated.
32 devices in a mesh: node: 4 (over z), wide: 8 (over y, x, core).
Axes of the slice: x: 2, y: 2, z: 4, core: 2. Of those that a mesh axis runs over, the one named last changes fastest.
Arguments:
- tokens: bfloat16 [16384, 768], P(('node', 'wide')), may hold values from -6 to 6
- expert_index: int32 [16384, 1], P(('node', 'wide')), may hold values from 0 to 63; in each aligned block of 512 rows (0 to 511, 512 to 1023, ...) at most 16 rows name the same one
- norm_gain: float32 [768], replicated, may hold values from 0.5 to 1.5
- router_weight: float32 [768, 64], replicated, may hold values from -0.21875 to 0.21875
- expert_in: bfloat16 [64, 768, 3072], P(('node', 'wide')), may hold values from -0.21875 to 0.21875
- expert_out: bfloat16 [64, 3072, 768], P(('node', 'wide')), may hold values from -0.109375 to 0.109375
- post_gain: float32 [768], replicated, may hold values from 0.5 to 1.5
- dense_in: bfloat16 [3072, 768], P('node'), may hold values from -0.21875 to 0.21875
- scale_in: float32 [3072], P('node'), may hold values from 0.5 to 2
- dense_out: bfloat16 [3072, 768], P('node'), may hold values from -0.109375 to 0.109375
- scale_out: float32 [768], replicated, may hold values from 0.5 to 2
Outputs:
- layer_out: bfloat16 [16384, 768], P(('node', 'wide'))
Inputs may be any that keep to these rules, and one draw needn't show every extreme that they name: `expert_index`: in each aligned block of 512 rows (the tokens of one device) no expert is named by more than 16 rows, a bound that some block reaches.
All inputs are finite; a program needn't handle non-finite values.
Results may differ from a plain program's by a relative error of at most 0.01.
Values may be sent and summed in bfloat16 or wider, within the bound.
A program may use at most 128 MiB of HBM per device.

v0:
```python
import jax
import jax.numpy as jnp
from jax import lax
from jax.sharding import PartitionSpec as P


def root_norm(values, gain_vector):
    floats = values.astype(jnp.float32)
    square_mean = jnp.mean(floats * floats, axis=-1, keepdims=True)
    return (floats * lax.rsqrt(square_mean + 1e-06) * gain_vector).astype(jnp.bfloat16)


def per_device(
    tokens,
    expert_index,
    norm_gain,
    router_weight,
    expert_in,
    expert_out,
    post_gain,
    dense_in,
    scale_in,
    dense_out,
    scale_out,
):
    tok_dev = tokens.shape[0]
    model_width = tokens.shape[1]
    experts = router_weight.shape[1]
    held_experts = expert_in.shape[0]
    devices = experts // held_experts
    capacity = max(2, 2 * tok_dev // experts)
    total_rows = experts * capacity
    normed = root_norm(tokens, norm_gain)
    chosen = expert_index[:, 0]
    columns = lax.broadcasted_iota(jnp.int32, (tok_dev, experts), 1)
    picked = chosen[:, None] == columns
    logits = jnp.dot(normed.astype(jnp.float32), router_weight, precision=lax.Precision.HIGHEST)
    picked_logit = jnp.sum(jnp.where(picked, logits, 0.0), axis=1)
    gate_prob = 1.0 / (1.0 + jnp.exp(-picked_logit))
    onehot = picked.astype(jnp.bfloat16)
    earlier = (
        lax.broadcasted_iota(jnp.int32, (tok_dev, tok_dev), 0)
        > lax.broadcasted_iota(jnp.int32, (tok_dev, tok_dev), 1)
    ).astype(jnp.bfloat16)
    before = jnp.dot(earlier, onehot, preferred_element_type=jnp.float32)
    slot_index = jnp.sum(jnp.where(picked, before, 0.0), axis=1).astype(jnp.int32)
    position = (
        chosen % held_experts * (devices * capacity)
        + chosen // held_experts * capacity
        + slot_index
    )
    dispatch = (
        lax.broadcasted_iota(jnp.int32, (total_rows, tok_dev), 0) == position[None, :]
    ).astype(jnp.bfloat16)
    outgoing = jnp.dot(dispatch, normed, preferred_element_type=jnp.float32).astype(jnp.bfloat16)
    packed = outgoing.reshape(held_experts, devices, capacity, model_width)
    arrived_rows = lax.all_to_all(packed, ("node", "wide"), split_axis=1, concat_axis=1, tiled=True)
    flat_rows = arrived_rows.reshape(held_experts, -1, model_width)
    hidden = jnp.einsum("jrd,jdf->jrf", flat_rows, expert_in, preferred_element_type=jnp.float32)
    hidden = jax.nn.relu(hidden).astype(jnp.bfloat16)
    produced = jnp.einsum("jrf,jfd->jrd", hidden, expert_out, preferred_element_type=jnp.float32)
    returned = lax.all_to_all(
        produced.astype(jnp.bfloat16).reshape(arrived_rows.shape),
        ("node", "wide"),
        split_axis=1,
        concat_axis=1,
        tiled=True,
    )
    expert_result = jnp.take(returned.reshape(total_rows, model_width), position, axis=0)
    residual = (
        tokens.astype(jnp.float32) + gate_prob[:, None] * expert_result.astype(jnp.float32)
    ).astype(jnp.bfloat16)
    normed2 = root_norm(residual, post_gain)
    gathered = lax.all_gather(normed2, "node", axis=0, tiled=True)
    projected = lax.dot_general(
        gathered, dense_in, (((1,), (1,)), ((), ())), preferred_element_type=jnp.float32
    )
    hidden_part = jax.nn.relu(projected * scale_in[None, :]).astype(jnp.bfloat16)
    dense_sum = lax.psum_scatter(
        jnp.dot(hidden_part, dense_out, preferred_element_type=jnp.float32).astype(jnp.bfloat16),
        "node",
        scatter_dimension=0,
        tiled=True,
    ).astype(jnp.float32)
    return (residual.astype(jnp.float32) + dense_sum * scale_out[None, :]).astype(jnp.bfloat16)


def solution(mesh):
    return jax.shard_map(
        per_device,
        mesh=mesh,
        in_specs=(
            P(("node", "wide"), None),
            P(("node", "wide"), None),
            P(),
            P(),
            P(("node", "wide"), None, None),
            P(("node", "wide"), None, None),
            P(),
            P("node", None),
            P("node"),
            P("node", None),
            P(),
        ),
        out_specs=P(("node", "wide"), None),
        check_vma=False,
    )
```

profile of v0, /device:TPU:0, one launch (start us, length us, event | category | flops | bytes accessed | tf_op | source)
XLA Modules:
  0.0 256.8 jit_solution(18025031928886057892)
XLA Ops:
  6.5 1.1 fusion.11
  7.6 0.7 fusion.18
  8.3 1.4 fusion.2
  9.7 2.3 fusion.1
  12.0 0.0 copy-start.5
  12.0 0.2 copy.15
  12.3 45.1 %all_to_all.10 = bf16[2,32,16,768]{3,2,0,1:T(8,128)(2,1)S(1)} all-to-all(bf16[2,32,16,768]{3,2,0,1:T(8,128)(2,1)S(1)} %copy.15), channel_id=1, replica_groups=mesh['node'=4,'wide'=8] {'node','wide'}, dimensions={1} | all-to-all | bytes 3145728 | tf_op jit(solution)/shard_map/all_to_all | solution.py:57
  57.4 0.1 copy.16
  57.5 0.0 slice-start.1
  57.5 0.0 slice-start.2
  57.5 5.3 %maximum_convert_fusion = bf16[2,512,3072]{2,1,0:T(8,128)(2,1)S(1)} fusion(bf16[2,512,768]{2,1,0:T(8,128)(2,1)S(1)} %bitcast.17, bf16[2,768,3072]{2,1,0:T(8,128)(2,1)S(1)} %copy-done.5), kind=kOutput, calls=%fused_computation.1 | convolution fusion | flops 4838129664 | bytes 17301504 | tf_op jit(solution)/shard_map/jrd,jdf->jrf/dot_general | solution.py:59
  62.8 0.0 slice-done
  62.8 0.0 slice-done.1
  62.8 5.1 %convolution_convert_fusion.1 = bf16[2,512,768]{2,1,0:T(8,128)(2,1)S(1)} fusion(bf16[2,512,3072]{2,1,0:T(8,128)(2,1)S(1)} %maximum_convert_fusion, bf16[2,3072,768]{2,1,0:T(8,128)(2,1)S(1)} %bitcast.25), kind=kOutput, calls=%fused_computation.13 | convolution fusion | flops 4832624640 | bytes 17301504 | tf_op jit(solution)/shard_map/jrf,jfd->jrd/dot_general | solution.py:61
  68.0 1.3 copy.17
  69.3 3.6 %all-to-all-start.1 = ((bf16[2,32,16,768]{3,2,0,1:T(8,128)(2,1)}), bf16[2,32,16,768]{3,2,0,1:T(8,128)(2,1)}, u32[]{:S(2)}, u32[]{:S(2)}) async-start(bf16[2,32,16,768]{3,2,0,1:T(8,128)(2,1)} %copy.17), calls=%async_computation.1 | async-start | bytes 3145728 | tf_op jit(solution)/shard_map/all_to_all | solution.py:62
  72.9 0.0 all-gather.2.cloned.1.call-start
  73.0 0.9 fusion.10
  74.0 36.7 %all-to-all-done.1 = bf16[2,32,16,768]{3,2,0,1:T(8,128)(2,1)} async-done(((bf16[2,32,16,768]{3,2,0,1:T(8,128)(2,1)}), bf16[2,32,16,768]{3,2,0,1:T(8,128)(2,1)}, u32[]{:S(2)}, u32[]{:S(2)}) %all-to-all-start.1) | async-done | bytes 1572896 | tf_op jit(solution)/shard_map/all_to_all | solution.py:62
  110.7 1.5 copy.18
  112.2 2.7 %gather_fusion = bf16[512,768]{1,0:T(8,128)(2,1)} fusion(bf16[1024,768]{1,0:T(8,128)(2,1)S(1)} %bitcast.15, s32[1024]{0:T(1024)S(1)} %pad_clamp_fusion), kind=kCustom, calls=%fused_computation | custom fusion | bytes 1574912 | tf_op jit(solution)/shard_map/jit(_take)/gather | solution.py:69
  114.9 1.7 fusion.6
  116.7 0.0 copy-start.6
  116.7 0.0 copy-start.9
  116.7 1.1 fusion.8
  117.8 0.0 all-gather.2.cloned.1.call-update
  117.9 0.0 reduce-scatter.2.cloned.1.call-start
  117.9 62.6 %all-gather.2.cloned.1.call-done = bf16[2048,768]{1,0:T(8,128)(2,1)} async-done(((bf16[512,768]{1,0:T(8,128)(2,1)}), bf16[2048,768]{1,0:T(8,128)(2,1)}) %all-gather.2.cloned.1.call-update) | async-done | bytes 3145744 | tf_op jit(solution)/shard_map/all_gather | solution.py:74
  180.5 8.1 %convolution_convert_fusion = bf16[2048,768]{1,0:T(8,128)(2,1)} fusion(bf16[768,768]{1,0:T(8,128)(2,1)S(1)} %copy-done, bf16[2048,768]{1,0:T(8,128)(2,1)} %all-gather.2.cloned.1.call-done, bf16[768,768]{1,0:T(8,128)(2,1)S(1)} %copy-done.6, f32[768]{0:T(1024)S(1)} %copy-done.9), kind=kOutput, calls=%fused_computation.3 | convolution fusion | flops 4838129664 | bytes 8653824 | tf_op jit(solution)/shard_map/dot_general | solution.py:80
  188.6 0.0 reduce-scatter.2.cloned.1.call-update
  188.6 59.1 %reduce-scatter.2.cloned.1.call-done = bf16[512,768]{1,0:T(8,128)(2,1)} async-done(((bf16[2048,768]{1,0:T(8,128)(2,1)}), bf16[512,768]{1,0:T(8,128)(2,1)}) %reduce-scatter.2.cloned.1.call-update) | async-done | bytes 786448 | tf_op jit(solution)/shard_map/reduce_scatter | solution.py:79
  247.7 2.2 fusion.9
  (26 shorter events, 0.1 us)
Async XLA Ops:
  6.5 173.9 %copy-start = (bf16[768,768]{1,0:T(8,128)(2,1)S(1)}, bf16[768,768]{1,0:T(8,128)(2,1)}, u32[]{:S(2)}) copy-start(bf16[768,768]{1,0:T(8,128)(2,1)} %param.20) | copy-start | bytes 3538948
  12.0 45.5 %copy-start.5 = (bf16[2,768,3072]{2,1,0:T(8,128)(2,1)S(1)}, bf16[2,768,3072]{2,1,0:T(8,128)(2,1)}, u32[]{:S(2)}) copy-start(bf16[2,768,3072]{2,1,0:T(8,128)(2,1)} %param.15) | copy-start | bytes 28311556
  57.4 5.4 %slice-start = ((s8[9437184]{0:T(1024)(128)(4,1)}), s8[4194304]{0:T(1024)(128)(4,1)S(1)}, s32[]{:S(2)}) async-start(s8[9437184]{0:T(1024)(128)(4,1)} %bitcast.24), calls=%async_computation.5 | async-start | bytes 8388608
  57.5 5.3 %slice-start.1 = ((s8[9437184]{0:T(1024)(128)(4,1)}), s8[4194304]{0:T(1024)(128)(4,1)S(1)}, s32[]{:S(2)}) async-start(s8[9437184]{0:T(1024)(128)(4,1)} %bitcast.24), calls=%async_computation.6 | async-start | bytes 8388608
  57.5 5.3 %slice-start.2 = ((s8[9437184]{0:T(1024)(128)(4,1)}), s8[1048576]{0:T(1024)(128)(4,1)S(1)}, s32[]{:S(2)}) async-start(s8[9437184]{0:T(1024)(128)(4,1)} %bitcast.24), calls=%async_computation.7 | async-start | bytes 2097152
  69.3 3.6 %copy-start.2 = (s32[512,1]{0,1:T(1,128)S(1)}, s32[512,1]{0,1:T(1,128)}, u32[]{:S(2)}) copy-start(s32[512,1]{0,1:T(1,128)} %param.12) | copy-start | bytes 6148
  69.3 3.7 %copy-start.1 = (bf16[512,768]{1,0:T(8,128)(2,1)S(1)}, bf16[512,768]{1,0:T(8,128)(2,1)}, u32[]{:S(2)}) copy-start(bf16[512,768]{1,0:T(8,128)(2,1)} %param.11) | copy-start | bytes 2359300
  69.3 3.7 %copy-start.7 = (f32[768,64]{0,1:T(8,128)S(1)}, f32[768,64]{0,1:T(8,128)}, u32[]{:S(2)}) copy-start(f32[768,64]{0,1:T(8,128)} %param.14) | copy-start | bytes 589828
  69.3 3.7 %copy-start.8 = (f32[768]{0:T(1024)S(1)}, f32[768]{0:T(1024)}, u32[]{:S(2)}) copy-start(f32[768]{0:T(1024)} %param.13) | copy-start | bytes 9220
  69.3 41.4 %all-to-all-start.1 = ((bf16[2,32,16,768]{3,2,0,1:T(8,128)(2,1)}), bf16[2,32,16,768]{3,2,0,1:T(8,128)(2,1)}, u32[]{:S(2)}, u32[]{:S(2)}) async-start(bf16[2,32,16,768]{3,2,0,1:T(8,128)(2,1)} %copy.17), calls=%async_computation.1 | async-start | bytes 3145728 | tf_op jit(solution)/shard_map/all_to_all | solution.py:62
  72.9 107.6 %all-gather.2.cloned.1.call-start = ((), (), s32[]{:S(2)}) async-start(), calls=%async_computation.3 | async-start | bytes 3932160 | tf_op jit(solution)/shard_map/all_gather | solution.py:74
  114.9 1.8 copy-start.3
  116.7 63.8 %copy-start.6 = (bf16[768,768]{1,0:T(8,128)(2,1)S(1)}, bf16[768,768]{1,0:T(8,128)(2,1)}, u32[]{:S(2)}) copy-start(bf16[768,768]{1,0:T(8,128)(2,1)} %param.18) | copy-start | bytes 3538948
  116.7 63.8 %copy-start.9 = (f32[768]{0:T(1024)S(1)}, f32[768]{0:T(1024)}, u32[]{:S(2)}) copy-start(f32[768]{0:T(1024)} %param.19) | copy-start | bytes 9220
  117.9 129.8 %reduce-scatter.2.cloned.1.call-start = ((), (), s32[]{:S(2)}) async-start(), calls=%async_computation.4 | async-start | bytes 3932160 | tf_op jit(solution)/shard_map/reduce_scatter | solution.py:79
  188.6 59.1 %copy-start.4 = (f32[768]{0:T(1024)S(1)}, f32[768]{0:T(1024)}, u32[]{:S(2)}) copy-start(f32[768]{0:T(1024)} %param.21) | copy-start | bytes 9220
Sparse Core Ops, SparseCore 0:
  118.0 62.4 all-gather.1
  188.7 58.8 reduce-scatter.1
where the time goes:
time: 257 us
  waiting for transfers between devices  158 us (61%)
  blocking collectives  45.1 us (18%)
  matrix products  22.8 us (9%)
  between operations  13.6 us (5%)
  other arithmetic  7.22 us (3%)
  local copies, waits for them, and re-layouts  5.95 us (2%)
  starting transfers between devices  3.65 us (1%)
    all_gather x1, waiting for transfers between devices, per_device(): gathered = lax.all_gather(normed2, 'node', axis=0, tiled=True)  62.6 us
    reduce_scatter x1, waiting for transfers between devices, per_device(): lax.psum_scatter(jnp.dot(hidden_part, dense_out, preferred_element_type=j...  59.1 us
    all_to_all x1, blocking collectives, per_device(): lax.all_to_all(packed, ('node', 'wide'), split_axis=1, concat_axis=1, til...  45.1 us
    all_to_all x1, waiting for transfers between devices, per_device(): lax.all_to_all(produced.astype(jnp.bfloat16).reshape(arrived_rows.shape),...  36.7 us
    dot_general x1, matrix products, per_device(): jnp.dot(hidden_part, dense_out, preferred_element_type=jnp.float32)  8.1 us
    dot_general x1, matrix products, per_device(): jnp.einsum('jrd,jdf->jrf', flat_rows, expert_in, preferred_element_type=j...  5.27 us
  transfers between devices with their start and end apart: 3, of which 3 were waited for; matrix products, arithmetic and copies ran while one was open for 0% of the time, Pallas kernels for 0%

commit v1 on v0

--- a/solution.py
+++ b/solution.py
@@ -8,6 +8,12 @@
     floats = values.astype(jnp.float32)
     square_mean = jnp.mean(floats * floats, axis=-1, keepdims=True)
     return (floats * lax.rsqrt(square_mean + 1e-06) * gain_vector).astype(jnp.bfloat16)
+
+
+def gather_codes(codes):
+    part = codes.shape[0] // lax.axis_size("wide")
+    own = lax.dynamic_slice_in_dim(codes, lax.axis_index("wide") * part, part, 0)
+    return lax.all_gather(own, ("node", "wide"), axis=0, tiled=True)
 
 
 def per_device(
@@ -23,6 +29,9 @@
     dense_out,
     scale_out,
 ):
+    full_in = gather_codes(dense_in)
+    full_out = gather_codes(dense_out)
+    full_scale = lax.all_gather(scale_in, "node", axis=0, tiled=True)
     tok_dev = tokens.shape[0]
     model_width = tokens.shape[1]
     experts = router_weight.shape[1]
@@ -71,17 +80,11 @@
         tokens.astype(jnp.float32) + gate_prob[:, None] * expert_result.astype(jnp.float32)
     ).astype(jnp.bfloat16)
     normed2 = root_norm(residual, post_gain)
-    gathered = lax.all_gather(normed2, "node", axis=0, tiled=True)
     projected = lax.dot_general(
-        gathered, dense_in, (((1,), (1,)), ((), ())), preferred_element_type=jnp.float32
+        normed2, full_in, (((1,), (1,)), ((), ())), preferred_element_type=jnp.float32
     )
-    hidden_part = jax.nn.relu(projected * scale_in[None, :]).astype(jnp.bfloat16)
-    dense_sum = lax.psum_scatter(
-        jnp.dot(hidden_part, dense_out, preferred_element_type=jnp.float32).astype(jnp.bfloat16),
-        "node",
-        scatter_dimension=0,
-        tiled=True,
-    ).astype(jnp.float32)
+    hidden_units = jax.nn.relu(projected * full_scale[None, :]).astype(jnp.bfloat16)
+    dense_sum = jnp.dot(hidden_units, full_out, preferred_element_type=jnp.float32)
     return (residual.astype(jnp.float32) + dense_sum * scale_out[None, :]).astype(jnp.bfloat16)
 
 

time: 257 us -> 173 us (0.67)
  waiting for transfers between devices: 158 us -> 12.3 us
  blocking collectives: 45.1 us -> 106 us
  local copies, waits for them, and re-layouts: 5.95 us -> 9.46 us
  other arithmetic: 7.22 us -> 3.83 us
    reduce_scatter x1 -> x0, waiting for transfers between devices: 59.1 us -> none  [per_device(): lax.psum_scatter(jnp.dot(hidden_part, dense_out, preferred_element_type=j...]
    all_gather x0 -> x1, blocking collectives: none -> 51.7 us  [per_device(): full_scale = lax.all_gather(scale_in, 'node', axis=0, tiled=True)]
    all_gather x1 -> x2, waiting for transfers between devices: 62.6 us -> 12.2 us  [gather_codes(): return lax.all_gather(own, ('node', 'wide'), axis=0, tiled=True)]
    all_to_all x1, waiting for transfers between devices: 36.7 us -> 0.01 us  [per_device(): lax.all_to_all(produced.astype(jnp.bfloat16).reshape(arrived_rows.shape),...]
    all_to_all x1, blocking collectives: 45.1 us -> 54.6 us  [per_device(): lax.all_to_all(packed, ('node', 'wide'), split_axis=1, concat_axis=1, til...]
    convert_element_type x2 -> x0, other arithmetic: 3.37 us -> none  [the longest x1 2.24 us: per_device(): (residual.astype(jnp.float32) + dense_sum * scale_out[None, :]).astype(jn...]
  transfers between devices with their start and end apart: 3 -> 3, of which waited for: 3 -> 1; matrix products, arithmetic and copies ran while one was open for 0% -> 14% of each run, Pallas kernels for 0% -> 0%
where the time goes in v1:
time: 173 us
  blocking collectives  106 us (61%)
  matrix products  23.5 us (14%)
  between operations  13.6 us (8%)
  waiting for transfers between devices  12.3 us (7%)
  local copies, waits for them, and re-layouts  9.46 us (5%)
  other arithmetic  3.83 us (2%)
  starting transfers between devices  3.59 us (2%)
    all_to_all x1, blocking collectives, per_device(): lax.all_to_all(packed, ('node', 'wide'), split_axis=1, concat_axis=1, til...  54.6 us
    all_gather x1, blocking collectives, per_device(): full_scale = lax.all_gather(scale_in, 'node', axis=0, tiled=True)  51.7 us
    all_gather x2, waiting for transfers between devices, gather_codes(): return lax.all_gather(own, ('node', 'wide'), axis=0, tiled=True)  12.2 us
    dot_general x1, matrix products, per_device(): jnp.dot(hidden_units, full_out, preferred_element_type=jnp.float32)  9.92 us
    dot_general x1, matrix products, per_device(): jnp.einsum('jrd,jdf->jrf', flat_rows, expert_in, preferred_element_type=j...  5.27 us
    dot_general x1, matrix products, per_device(): jnp.einsum('jrf,jfd->jrd', hidden, expert_out, preferred_element_type=jnp...  5.1 us
    all_to_all x1, starting transfers between devices, per_device(): lax.all_to_all(produced.astype(jnp.bfloat16).reshape(arrived_rows.shape),...  3.54 us
  transfers between devices with their start and end apart: 3, of which 1 were waited for; matrix products, arithmetic and copies ran while one was open for 14% of the time, Pallas kernels for 0%

profile of v1, /device:TPU:0, one launch (start us, length us, event | category | flops | bytes accessed | tf_op | source)
XLA Modules:
  0.0 172.5 jit_solution(10234697962762538487)
XLA Ops:
  6.6 1.3 copy-done
  7.8 0.7 constant_dynamic-slice_fusion.1
  8.5 0.0 all-gather.4.cloned.1.call-update
  8.5 0.0 all-gather.6.cloned.1.call-start
  8.5 1.6 constant_dynamic-slice_fusion
  10.1 0.0 all-gather.6.cloned.1.call-update
  10.2 1.0 fusion.11
  11.2 0.7 fusion.24
  11.9 0.2 fusion.2
  12.2 1.2 fusion.1
  13.4 0.0 copy-start.4
  13.4 0.2 copy.15
  13.6 54.6 %all_to_all.10 = bf16[2,32,16,768]{3,2,0,1:T(8,128)(2,1)S(1)} all-to-all(bf16[2,32,16,768]{3,2,0,1:T(8,128)(2,1)S(1)} %copy.15), channel_id=1, replica_groups=mesh['node'=4,'wide'=8] {'node','wide'}, dimensions={1} | all-to-all | bytes 3145728 | tf_op jit(solution)/shard_map/all_to_all | solution.py:66
  68.2 0.1 copy.16
  68.3 0.0 slice-start.1
  68.3 0.0 slice-start.2
  68.4 5.3 %maximum_convert_fusion = bf16[2,512,3072]{2,1,0:T(8,128)(2,1)S(1)} fusion(bf16[2,512,768]{2,1,0:T(8,128)(2,1)S(1)} %bitcast.17, bf16[2,768,3072]{2,1,0:T(8,128)(2,1)S(1)} %copy-done.4), kind=kOutput, calls=%fused_computation.1 | convolution fusion | flops 4838129664 | bytes 17301504 | tf_op jit(solution)/shard_map/jrd,jdf->jrf/dot_general | solution.py:68
  73.7 5.1 %convolution_convert_fusion = bf16[2,512,768]{2,1,0:T(8,128)(2,1)S(1)} fusion(bf16[2,512,3072]{2,1,0:T(8,128)(2,1)S(1)} %maximum_convert_fusion, bf16[2,3072,768]{2,1,0:T(8,128)(2,1)S(1)} %bitcast.26), kind=kOutput, calls=%fused_computation.12 | convolution fusion | flops 4832624640 | bytes 17301504 | tf_op jit(solution)/shard_map/jrf,jfd->jrd/dot_general | solution.py:70
  78.8 1.4 copy.17
  80.1 3.5 %all-to-all-start.1 = ((bf16[2,32,16,768]{3,2,0,1:T(8,128)(2,1)}), bf16[2,32,16,768]{3,2,0,1:T(8,128)(2,1)}, u32[]{:S(2)}, u32[]{:S(2)}) async-start(bf16[2,32,16,768]{3,2,0,1:T(8,128)(2,1)} %copy.17), calls=%async_computation.1 | async-start | bytes 3145728 | tf_op jit(solution)/shard_map/all_to_all | solution.py:71
  83.7 0.0 copy-done.3
  83.7 51.7 %all-gather = f32[4,1,768]{2,1,0:T(1,128)S(1)} all-gather(f32[1,1,768]{2,1,0:T(1,128)S(1)} %reshape.118), channel_id=1, replica_groups=mesh['node'=4,'wide'=8] {'node'}, dimensions={0}, use_global_device_ids=true | all-gather | bytes 15360 | tf_op jit(solution)/shard_map/all_gather | solution.py:34
  135.4 0.5 and_reduce_fusion
  136.0 0.9 fusion.10
  136.9 0.6 add_divide_fusion
  137.5 0.0 all-to-all-done.1
  137.5 1.5 copy.18
  139.1 2.7 %gather_fusion = bf16[512,768]{1,0:T(8,128)(2,1)} fusion(bf16[1024,768]{1,0:T(8,128)(2,1)S(1)} %bitcast.15, s32[1024]{0:T(1024)S(1)} %pad_clamp_fusion), kind=kCustom, calls=%fused_computation | custom fusion | bytes 1574912 | tf_op jit(solution)/shard_map/jit(_take)/gather | solution.py:78
  141.8 1.7 %fusion.6 = (f32[512]{0:T(512)S(1)}, bf16[512,768]{1,0:T(8,128)(2,1)S(1)}) fusion(bf16[512,768]{1,0:T(8,128)(2,1)} %gather_fusion, pred[512]{0:T(512)(128)(4,1)} %get-tuple-element.7, f32[512]{0:T(512)} %add_divide_fusion, bf16[512,768]{1,0:T(8,128)(2,1)S(1)} %copy-done.1), kind=kLoop, calls=%fused_computation.17 | loop fusion | flops 3538432 | bytes 2363904 | tf_op jit(solution)/shard_map/reduce_sum | solution.py:9
  143.5 0.0 all-gather.4.cloned.1.call-done
  143.5 12.2 %all-gather.6.cloned.1.call-done = bf16[3072,768]{1,0:T(8,128)(2,1)} async-done(((bf16[96,768]{1,0:T(8,128)(2,1)}), bf16[3072,768]{1,0:T(8,128)(2,1)}) %all-gather.6.cloned.1.call-update) | async-done | bytes 4718608 | tf_op jit(solution)/shard_map/all_gather | solution.py:16
  155.8 9.9 %fusion.9 = bf16[512,768]{1,0:T(8,128)(2,1)} fusion(bf16[512,768]{1,0:T(8,128)(2,1)S(1)} %get-tuple-element.6, bf16[3072,768]{1,0:T(8,128)(2,1)} %all-gather.6.cloned.1.call-done, bf16[3072,768]{1,0:T(8,128)(2,1)} %all-gather.4.cloned.1.call-done, f32[3072]{0:T(1024)S(1)} %bitcast.19, f32[768]{0:T(1024)S(1)} %copy-done.7, f32[768]{0:T(1024)S(1)} %copy-done.8, ...), kind=kOutput, calls=%fused_computation.20 | convolution fusion | flops 4839702528 | bytes 11030528 | tf_op jit(solution)/shard_map/dot_general | solution.py:87
  (26 shorter events, 0.1 us)
Async XLA Ops:
  6.5 1.3 copy-start
  6.5 5.4 %copy-start.1 = (bf16[512,768]{1,0:T(8,128)(2,1)S(1)}, bf16[512,768]{1,0:T(8,128)(2,1)}, u32[]{:S(2)}) copy-start(bf16[512,768]{1,0:T(8,128)(2,1)} %param.11) | copy-start | bytes 2359300
  6.5 5.6 %copy-start.6 = (f32[768]{0:T(1024)S(1)}, f32[768]{0:T(1024)}, u32[]{:S(2)}) copy-start(f32[768]{0:T(1024)} %param.13) | copy-start | bytes 9220
  6.5 137.0 %all-gather.4.cloned.1.call-start = ((), (), s32[]{:S(2)}) async-start(), calls=%async_computation.2 | async-start | bytes 4866048 | tf_op jit(solution)/shard_map/all_gather | solution.py:16
  8.5 147.3 %all-gather.6.cloned.1.call-start = ((), (), s32[]{:S(2)}) async-start(), calls=%async_computation.3 | async-start | bytes 4866048 | tf_op jit(solution)/shard_map/all_gather | solution.py:16
  13.4 55.0 %copy-start.4 = (bf16[2,768,3072]{2,1,0:T(8,128)(2,1)S(1)}, bf16[2,768,3072]{2,1,0:T(8,128)(2,1)}, u32[]{:S(2)}) copy-start(bf16[2,768,3072]{2,1,0:T(8,128)(2,1)} %param.15) | copy-start | bytes 28311556
  68.2 5.4 %slice-start = ((s8[9437184]{0:T(1024)(128)(4,1)}), s8[4194304]{0:T(1024)(128)(4,1)S(1)}, s32[]{:S(2)}) async-start(s8[9437184]{0:T(1024)(128)(4,1)} %bitcast.25), calls=%async_computation.4 | async-start | bytes 8388608
  68.3 5.3 %slice-start.1 = ((s8[9437184]{0:T(1024)(128)(4,1)}), s8[4194304]{0:T(1024)(128)(4,1)S(1)}, s32[]{:S(2)}) async-start(s8[9437184]{0:T(1024)(128)(4,1)} %bitcast.25), calls=%async_computation.5 | async-start | bytes 8388608
  68.3 5.3 %slice-start.2 = ((s8[9437184]{0:T(1024)(128)(4,1)}), s8[1048576]{0:T(1024)(128)(4,1)S(1)}, s32[]{:S(2)}) async-start(s8[9437184]{0:T(1024)(128)(4,1)} %bitcast.25), calls=%async_computation.6 | async-start | bytes 2097152
  80.1 3.6 %copy-start.3 = (f32[768]{0:T(1024)S(1)}, f32[768]{0:T(1024)}, u32[]{:S(2)}) copy-start(f32[768]{0:T(1024)} %param.19) | copy-start | bytes 9220
  80.1 55.3 %copy-start.2 = (s32[512,1]{0,1:T(1,128)S(1)}, s32[512,1]{0,1:T(1,128)}, u32[]{:S(2)}) copy-start(s32[512,1]{0,1:T(1,128)} %param.12) | copy-start | bytes 6148
  80.1 55.8 %copy-start.5 = (f32[768,64]{0,1:T(8,128)S(1)}, f32[768,64]{0,1:T(8,128)}, u32[]{:S(2)}) copy-start(f32[768,64]{0,1:T(8,128)} %param.14) | copy-start | bytes 589828
  80.1 57.4 %all-to-all-start.1 = ((bf16[2,32,16,768]{3,2,0,1:T(8,128)(2,1)}), bf16[2,32,16,768]{3,2,0,1:T(8,128)(2,1)}, u32[]{:S(2)}, u32[]{:S(2)}) async-start(bf16[2,32,16,768]{3,2,0,1:T(8,128)(2,1)} %copy.17), calls=%async_computation.1 | async-start | bytes 3145728 | tf_op jit(solution)/shard_map/all_to_all | solution.py:71
  141.8 14.0 %copy-start.7 = (f32[768]{0:T(1024)S(1)}, f32[768]{0:T(1024)}, u32[]{:S(2)}) copy-start(f32[768]{0:T(1024)} %param.21) | copy-start | bytes 9220
  141.8 14.0 %copy-start.8 = (f32[768]{0:T(1024)S(1)}, f32[768]{0:T(1024)}, u32[]{:S(2)}) copy-start(f32[768]{0:T(1024)} %param.17) | copy-start | bytes 9220
Sparse Core Ops, SparseCore 0:
  10.3 74.9 all-gather.3
  88.1 67.5 all-gather.5

commit v2 on v1

--- a/solution.py
+++ b/solution.py
@@ -10,10 +10,26 @@
     return (floats * lax.rsqrt(square_mean + 1e-06) * gain_vector).astype(jnp.bfloat16)
 
 
+def gather_scale(scale):
+    nodes = lax.axis_size("node")
+    me = lax.axis_index("node")
+    whole = jnp.zeros((nodes, scale.shape[0]), scale.dtype)
+    for hop in range(nodes):
+        block = scale
+        if hop > 0:
+            block = lax.ppermute(
+                scale, "node", [(source, (source + hop) % nodes) for source in range(nodes)]
+            )
+        whole = lax.dynamic_update_slice_in_dim(whole, block[None], (me - hop) % nodes, 0)
+    return whole
+
+
 def gather_codes(codes):
-    part = codes.shape[0] // lax.axis_size("wide")
+    wide = lax.axis_size("wide")
+    part = codes.shape[0] // wide
     own = lax.dynamic_slice_in_dim(codes, lax.axis_index("wide") * part, part, 0)
-    return lax.all_gather(own, ("node", "wide"), axis=0, tiled=True)
+    column = lax.all_gather(own, "node", axis=0, tiled=True)
+    return lax.all_gather(column, "wide", axis=0, tiled=True)
 
 
 def per_device(
@@ -31,7 +47,9 @@
 ):
     full_in = gather_codes(dense_in)
     full_out = gather_codes(dense_out)
-    full_scale = lax.all_gather(scale_in, "node", axis=0, tiled=True)
+    wide = lax.axis_size("wide")
+    scale_parts = gather_scale(scale_in).reshape(lax.axis_size("node"), wide, -1)
+    full_scale = scale_parts.transpose(1, 0, 2).reshape(-1)
     tok_dev = tokens.shape[0]
     model_width = tokens.shape[1]
     experts = router_weight.shape[1]

time: 173 us -> 168 us (0.971)
  blocking collectives: 106 us -> 66.7 us
  waiting for transfers between devices: 12.3 us -> 30.3 us
  starting transfers between devices: 3.59 us -> 16.8 us
  matrix products: 23.5 us -> 26.7 us
    all_to_all x1 -> x0, blocking collectives: 54.6 us -> none  [per_device(): lax.all_to_all(packed, ('node', 'wide'), split_axis=1, concat_axis=1, til...]
    ppermute x0 -> x3, waiting for transfers between devices: none -> 30.2 us  [gather_scale(): lax.ppermute(scale, 'node', [(source, (source + hop) % nodes) for source...]
    all_gather x1 -> x2, blocking collectives: 51.7 us -> 66.7 us  [gather_codes(): column = lax.all_gather(own, 'node', axis=0, tiled=True)]
    all_gather x2, waiting for transfers between devices: 12.2 us -> 0.04 us  [gather_codes(): return lax.all_gather(column, 'wide', axis=0, tiled=True)]
    all_to_all x0 -> x1, starting transfers between devices: none -> 6.36 us  [per_device(): lax.all_to_all(packed, ('node', 'wide'), split_axis=1, concat_axis=1, til...]
    ppermute x0 -> x3, starting transfers between devices: none -> 5.59 us  [gather_scale(): lax.ppermute(scale, 'node', [(source, (source + hop) % nodes) for source...]
    dot_general x1, matrix products: 5.27 us -> 9.24 us  [per_device(): jnp.einsum('jrd,jdf->jrf', flat_rows, expert_in, preferred_element_type=j...]
  transfers between devices with their start and end apart: 3 -> 7, of which waited for: 1 -> 2; matrix products, arithmetic and copies ran while one was open for 14% -> 17% of each run, Pallas kernels for 0% -> 0%
where the time goes in v2:
time: 168 us; the launch traced here: 167 us
  blocking collectives  66.7 us (40%)
  waiting for transfers between devices  30.3 us (18%)
  matrix products  26.7 us (16%)
  starting transfers between devices  16.8 us (10%)
  between operations  13.7 us (8%)
  local copies, waits for them, and re-layouts  9.77 us (6%)
  other arithmetic  3.22 us (2%)
    all_gather x2, blocking collectives, gather_codes(): column = lax.all_gather(own, 'node', axis=0, tiled=True)  66.7 us
    ppermute x3, waiting for transfers between devices, gather_scale(): lax.ppermute(scale, 'node', [(source, (source + hop) % nodes) for source...  30.2 us
    dot_general x1, matrix products, per_device(): jnp.dot(hidden_units, full_out, preferred_element_type=jnp.float32)  9.92 us
    dot_general x1, matrix products, per_device(): jnp.einsum('jrd,jdf->jrf', flat_rows, expert_in, preferred_element_type=j...  9.24 us
    all_to_all x1, starting transfers between devices, per_device(): lax.all_to_all(packed, ('node', 'wide'), split_axis=1, concat_axis=1, til...  6.36 us
    ppermute x3, starting transfers between devices, gather_scale(): lax.ppermute(scale, 'node', [(source, (source + hop) % nodes) for source...  5.59 us
    dot_general x1, matrix products, per_device(): jnp.einsum('jrf,jfd->jrd', hidden, expert_out, preferred_element_type=jnp...  5.1 us
    all_to_all x1, starting transfers between devices, per_device(): lax.all_to_all(produced.astype(jnp.bfloat16).reshape(arrived_rows.shape),...  4.78 us
  transfers between devices with their start and end apart: 7, of which 2 were waited for; matrix products, arithmetic and copies ran while one was open for 17% of the time, Pallas kernels for 0%

profile of v2, /device:TPU:0, one launch (start us, length us, event | category | flops | bytes accessed | tf_op | source)
XLA Modules:
  0.0 167.2 jit_solution(5029478986656258892)
XLA Ops:
  6.5 0.0 all-gather.3.cloned.1.call-start
  6.6 1.2 copy-done
  7.8 18.4 %all_gather.12 = bf16[384,768]{1,0:T(8,128)(2,1)} all-gather(bf16[96,768]{1,0:T(8,128)(2,1)S(1)} %constant_dynamic-slice_fusion.1), channel_id=1, replica_groups=mesh['node'=4,'wide'=8] {'node'}, dimensions={0}, use_global_device_ids=true | all-gather | bytes 737280 | tf_op jit(solution)/shard_map/all_gather | solution.py:31
  26.3 0.3 fusion.11
  26.6 0.2 fusion.2
  26.8 1.2 fusion.1
  28.1 1.3 copy.13
  29.4 6.4 %all-to-all-start = ((bf16[2,32,16,768]{3,2,0,1:T(8,128)(2,1)}), bf16[2,32,16,768]{3,2,0,1:T(8,128)(2,1)S(1)}, u32[]{:S(2)}, u32[]{:S(2)}) async-start(bf16[2,32,16,768]{3,2,0,1:T(8,128)(2,1)} %copy.13), calls=%async_computation | async-start | bytes 3145728 | tf_op jit(solution)/shard_map/all_to_all | solution.py:84
  35.7 0.0 all-gather.5.cloned.1.call-start
  35.8 0.9 constant_dynamic-slice_fusion
  36.7 48.3 %all_gather.14 = bf16[384,768]{1,0:T(8,128)(2,1)} all-gather(bf16[96,768]{1,0:T(8,128)(2,1)S(1)} %constant_dynamic-slice_fusion), channel_id=1, replica_groups=mesh['node'=4,'wide'=8] {'node'}, dimensions={0}, use_global_device_ids=true | all-gather | bytes 737280 | tf_op jit(solution)/shard_map/all_gather | solution.py:31
  85.0 0.1 copy.14
  85.2 9.2 %maximum_convert_fusion = bf16[2,512,3072]{2,1,0:T(8,128)(2,1)S(1)} fusion(bf16[2,512,768]{2,1,0:T(8,128)(2,1)S(1)} %bitcast.17, bf16[2,768,3072]{2,1,0:T(8,128)(2,1)} %param.15), kind=kOutput, calls=%fused_computation.1 | convolution fusion | flops 4838129664 | bytes 17301504 | tf_op jit(solution)/shard_map/jrd,jdf->jrf/dot_general | solution.py:86
  94.5 5.1 %convolution_convert_fusion = bf16[2,512,768]{2,1,0:T(8,128)(2,1)S(1)} fusion(bf16[2,512,3072]{2,1,0:T(8,128)(2,1)S(1)} %maximum_convert_fusion, bf16[2,3072,768]{2,1,0:T(8,128)(2,1)S(1)} %bitcast.26), kind=kOutput, calls=%fused_computation.12 | convolution fusion | flops 4832624640 | bytes 17301504 | tf_op jit(solution)/shard_map/jrf,jfd->jrd/dot_general | solution.py:88
  99.6 1.4 copy.15
  100.9 4.8 %all-to-all-start.1 = ((bf16[2,32,16,768]{3,2,0,1:T(8,128)(2,1)}), bf16[2,32,16,768]{3,2,0,1:T(8,128)(2,1)}, u32[]{:S(2)}, u32[]{:S(2)}) async-start(bf16[2,32,16,768]{3,2,0,1:T(8,128)(2,1)} %copy.15), calls=%async_computation.1 | async-start | bytes 3145728 | tf_op jit(solution)/shard_map/all_to_all | solution.py:89
  105.7 1.8 %collective-permute-start = (f32[768]{0:T(1024)S(1)}, f32[768]{0:T(1024)S(1)}, u32[]{:S(2)}, u32[]{:S(2)}) collective-permute-start(f32[768]{0:T(1024)S(1)} %copy-done.3), channel_id=1, source_target_pairs={{0,8},{8,16},{16,24},{24,0},{1,9},{9,17},{17,25},{25,1},{2,10},{10... | collective-permute-start | bytes 9224 | tf_op jit(solution)/shard_map/ppermute | solution.py:20
  107.5 2.4 %collective-permute-start.1 = (f32[768]{0:T(1024)S(1)}, f32[768]{0:T(1024)S(1)}, u32[]{:S(2)}, u32[]{:S(2)}) collective-permute-start(f32[768]{0:T(1024)S(1)} %copy-done.3), channel_id=1, source_target_pairs={{0,16},{8,24},{16,0},{24,8},{1,17},{9,25},{17,1},{25,9},{2,18},{10... | collective-permute-start | bytes 9224 | tf_op jit(solution)/shard_map/ppermute | solution.py:20
  109.9 1.4 collective-permute-start.2
  111.3 0.6 and_reduce_fusion
  111.9 0.9 fusion.10
  112.9 0.6 add_divide_fusion
  113.5 22.3 %collective-permute-done = f32[768]{0:T(1024)S(1)} collective-permute-done((f32[768]{0:T(1024)S(1)}, f32[768]{0:T(1024)S(1)}, u32[]{:S(2)}, u32[]{:S(2)}) %collective-permute-start) | collective-permute-done | bytes 3104 | tf_op jit(solution)/shard_map/ppermute | solution.py:20
  135.9 7.9 %collective-permute-done.1 = f32[768]{0:T(1024)S(1)} collective-permute-done((f32[768]{0:T(1024)S(1)}, f32[768]{0:T(1024)S(1)}, u32[]{:S(2)}, u32[]{:S(2)}) %collective-permute-start.1) | collective-permute-done | bytes 3104 | tf_op jit(solution)/shard_map/ppermute | solution.py:20
  143.9 0.2 dynamic_update_slice.15
  144.1 0.1 reshape.113
  144.2 0.1 mul.121
  144.3 1.5 copy.16
  145.9 2.7 %gather_fusion = bf16[512,768]{1,0:T(8,128)(2,1)} fusion(bf16[1024,768]{1,0:T(8,128)(2,1)S(1)} %bitcast.15, s32[1024]{0:T(1024)S(1)} %pad_clamp_fusion), kind=kCustom, calls=%fused_computation | custom fusion | bytes 1574912 | tf_op jit(solution)/shard_map/jit(_take)/gather | solution.py:96
  148.6 1.7 %fusion.6 = (f32[512]{0:T(512)S(1)}, bf16[512,768]{1,0:T(8,128)(2,1)S(1)}) fusion(bf16[512,768]{1,0:T(8,128)(2,1)} %gather_fusion, pred[512]{0:T(512)(128)(4,1)} %get-tuple-element.7, f32[512]{0:T(512)} %add_divide_fusion, bf16[512,768]{1,0:T(8,128)(2,1)S(1)} %copy-done.1), kind=kLoop, calls=%fused_computation.17 | loop fusion | flops 3538432 | bytes 2363904 | tf_op jit(solution)/shard_map/reduce_sum | solution.py:9
  150.3 0.0 all-gather.3.cloned.1.call-done
  150.4 9.9 %fusion.9 = bf16[512,768]{1,0:T(8,128)(2,1)} fusion(bf16[512,768]{1,0:T(8,128)(2,1)S(1)} %get-tuple-element.6, bf16[3072,768]{1,0:T(8,128)(2,1)} %all-gather.5.cloned.1.call-done, bf16[3072,768]{1,0:T(8,128)(2,1)} %all-gather.3.cloned.1.call-done, f32[3072]{0:T(1024)S(1)} %mul.121, f32[768]{0:T(1024)S(1)} %copy-done.6, f32[768]{0:T(1024)S(1)} %copy-done.7, ...), kind=kOutput, calls=%fused_computation.20 | convolution fusion | flops 4839702528 | bytes 11030528 | tf_op jit(solution)/shard_map/dot_general | solution.py:105
  (43 shorter events, 0.3 us)
Async XLA Ops:
  6.5 1.3 copy-start
  6.5 19.7 %copy-start.2 = (s32[512,1]{0,1:T(1,128)S(1)}, s32[512,1]{0,1:T(1,128)}, u32[]{:S(2)}) copy-start(s32[512,1]{0,1:T(1,128)} %param.12) | copy-start | bytes 6148
  6.5 20.0 %copy-start.1 = (bf16[512,768]{1,0:T(8,128)(2,1)S(1)}, bf16[512,768]{1,0:T(8,128)(2,1)}, u32[]{:S(2)}) copy-start(bf16[512,768]{1,0:T(8,128)(2,1)} %param.11) | copy-start | bytes 2359300
  6.5 20.3 %copy-start.5 = (f32[768]{0:T(1024)S(1)}, f32[768]{0:T(1024)}, u32[]{:S(2)}) copy-start(f32[768]{0:T(1024)} %param.13) | copy-start | bytes 9220
  6.5 143.8 %all-gather.3.cloned.1.call-start = ((), (), s32[]{:S(2)}) async-start(), calls=%async_computation.2 | async-start | bytes 5308416 | tf_op jit(solution)/shard_map/all_gather | solution.py:32
  29.4 55.6 %all-to-all-start = ((bf16[2,32,16,768]{3,2,0,1:T(8,128)(2,1)}), bf16[2,32,16,768]{3,2,0,1:T(8,128)(2,1)S(1)}, u32[]{:S(2)}, u32[]{:S(2)}) async-start(bf16[2,32,16,768]{3,2,0,1:T(8,128)(2,1)} %copy.13), calls=%async_computation | async-start | bytes 3145728 | tf_op jit(solution)/shard_map/all_to_all | solution.py:84
  35.7 114.6 %all-gather.5.cloned.1.call-start = ((), (), s32[]{:S(2)}) async-start(), calls=%async_computation.3 | async-start | bytes 5308416 | tf_op jit(solution)/shard_map/all_gather | solution.py:32
  85.0 9.4 %slice-start = ((s8[9437184]{0:T(1024)(128)(4,1)}), s8[4194304]{0:T(1024)(128)(4,1)S(1)}, s32[]{:S(2)}) async-start(s8[9437184]{0:T(1024)(128)(4,1)} %bitcast.25), calls=%async_computation.4 | async-start | bytes 8388608
  85.2 9.3 %slice-start.1 = ((s8[9437184]{0:T(1024)(128)(4,1)}), s8[4194304]{0:T(1024)(128)(4,1)S(1)}, s32[]{:S(2)}) async-start(s8[9437184]{0:T(1024)(128)(4,1)} %bitcast.25), calls=%async_computation.5 | async-start | bytes 8388608
  85.2 9.3 %slice-start.2 = ((s8[9437184]{0:T(1024)(128)(4,1)}), s8[1048576]{0:T(1024)(128)(4,1)S(1)}, s32[]{:S(2)}) async-start(s8[9437184]{0:T(1024)(128)(4,1)} %bitcast.25), calls=%async_computation.6 | async-start | bytes 2097152
  100.9 4.8 %copy-start.3 = (f32[768]{0:T(1024)S(1)}, f32[768]{0:T(1024)}, u32[]{:S(2)}) copy-start(f32[768]{0:T(1024)} %param.19) | copy-start | bytes 9220
  100.9 11.0 %copy-start.4 = (f32[768,64]{0,1:T(8,128)S(1)}, f32[768,64]{0,1:T(8,128)}, u32[]{:S(2)}) copy-start(f32[768,64]{0,1:T(8,128)} %param.14) | copy-start | bytes 589828
  100.9 43.4 %all-to-all-start.1 = ((bf16[2,32,16,768]{3,2,0,1:T(8,128)(2,1)}), bf16[2,32,16,768]{3,2,0,1:T(8,128)(2,1)}, u32[]{:S(2)}, u32[]{:S(2)}) async-start(bf16[2,32,16,768]{3,2,0,1:T(8,128)(2,1)} %copy.15), calls=%async_computation.1 | async-start | bytes 3145728 | tf_op jit(solution)/shard_map/all_to_all | solution.py:89
  105.7 30.1 %collective-permute-start = (f32[768]{0:T(1024)S(1)}, f32[768]{0:T(1024)S(1)}, u32[]{:S(2)}, u32[]{:S(2)}) collective-permute-start(f32[768]{0:T(1024)S(1)} %copy-done.3), channel_id=1, source_target_pairs={{0,8},{8,16},{16,24},{24,0},{1,9},{9,17},{17,25},{25,1},{2,10},{10... | collective-permute-start | bytes 9224 | tf_op jit(solution)/shard_map/ppermute | solution.py:20
  107.5 36.3 %collective-permute-start.1 = (f32[768]{0:T(1024)S(1)}, f32[768]{0:T(1024)S(1)}, u32[]{:S(2)}, u32[]{:S(2)}) collective-permute-start(f32[768]{0:T(1024)S(1)} %copy-done.3), channel_id=1, source_target_pairs={{0,16},{8,24},{16,0},{24,8},{1,17},{9,25},{17,1},{25,9},{2,18},{10... | collective-permute-start | bytes 9224 | tf_op jit(solution)/shard_map/ppermute | solution.py:20
  109.9 34.0 %collective-permute-start.2 = (f32[768]{0:T(1024)S(1)}, f32[768]{0:T(1024)S(1)}, u32[]{:S(2)}, u32[]{:S(2)}) collective-permute-start(f32[768]{0:T(1024)S(1)} %copy-done.3), channel_id=1, source_target_pairs={{0,24},{8,0},{16,8},{24,16},{1,25},{9,1},{17,9},{25,17},{2,26},{10... | collective-permute-start | bytes 9224 | tf_op jit(solution)/shard_map/ppermute | solution.py:20
  148.6 1.8 %copy-start.6 = (f32[768]{0:T(1024)S(1)}, f32[768]{0:T(1024)}, u32[]{:S(2)}) copy-start(f32[768]{0:T(1024)} %param.21) | copy-start | bytes 9220
  148.6 1.8 %copy-start.7 = (f32[768]{0:T(1024)S(1)}, f32[768]{0:T(1024)}, u32[]{:S(2)}) copy-start(f32[768]{0:T(1024)} %param.17) | copy-start | bytes 9220
Sparse Core Ops, SparseCore 0:
  26.4 56.4 all-gather.2
  85.1 52.4 all-gather.4

commit v3 on v2

--- a/solution.py
+++ b/solution.py
@@ -45,8 +45,8 @@
     dense_out,
     scale_out,
 ):
-    full_in = gather_codes(dense_in)
-    full_out = gather_codes(dense_out)
+    codes = gather_codes(jnp.concatenate([dense_in, dense_out], axis=1))
+    full_in, full_out = codes[:, : dense_in.shape[1]], codes[:, dense_in.shape[1] :]
     wide = lax.axis_size("wide")
     scale_parts = gather_scale(scale_in).reshape(lax.axis_size("node"), wide, -1)
     full_scale = scale_parts.transpose(1, 0, 2).reshape(-1)

time: 168 us -> 158 us (0.940)
  waiting for transfers between devices: 30.3 us -> 65 us
  blocking collectives: 66.7 us -> 41.5 us
  starting transfers between devices: 16.8 us -> 8.77 us
  local copies, waits for them, and re-layouts: 9.77 us -> 4.45 us
  matrix products: 26.7 us -> 21.5 us
    all_gather x2 -> x0, blocking collectives: 66.7 us -> none  [gather_codes(): column = lax.all_gather(own, 'node', axis=0, tiled=True)]
    all_to_all x0 -> x1, blocking collectives: none -> 41.5 us  [per_device(): lax.all_to_all(packed, ('node', 'wide'), split_axis=1, concat_axis=1, til...]
    all_gather x0 -> x1, waiting for transfers between devices: none -> 33.7 us  [gather_codes(): column = lax.all_gather(own, 'node', axis=0, tiled=True)]
    dot_general x1, matrix products: 9.92 us -> 3.53 us  [per_device(): jnp.dot(hidden_units, full_out, preferred_element_type=jnp.float32)]
    all_to_all x1 -> x0, starting transfers between devices: 6.36 us -> none  [per_device(): lax.all_to_all(packed, ('node', 'wide'), split_axis=1, concat_axis=1, til...]
    dot_general x0 -> x1, matrix products: none -> 5.16 us  [per_device(): lax.dot_general(normed2, full_in, (((1,), (1,)), ((), ())), preferred_ele...]
    dot_general x1, matrix products: 9.24 us -> 5.27 us  [per_device(): jnp.einsum('jrd,jdf->jrf', flat_rows, expert_in, preferred_element_type=j...]
    concatenate x0 -> x1, other arithmetic: none -> 1.77 us  [per_device(): codes = gather_codes(jnp.concatenate([dense_in, dense_out], axis=1))]
  transfers between devices with their start and end apart: 7 -> 6, of which waited for: 2 -> 3; matrix products, arithmetic and copies ran while one was open for 17% -> 11% of each run, Pallas kernels for 0% -> 0%
where the time goes in v3:
time: 158 us
  waiting for transfers between devices  65 us (41%)
  blocking collectives  41.5 us (26%)
  matrix products  21.5 us (14%)
  between operations  13.8 us (9%)
  starting transfers between devices  8.77 us (6%)
  local copies, waits for them, and re-layouts  4.45 us (3%)
  other arithmetic  2.68 us (2%)
    all_to_all x1, blocking collectives, per_device(): lax.all_to_all(packed, ('node', 'wide'), split_axis=1, concat_axis=1, til...  41.5 us
    all_gather x1, waiting for transfers between devices, gather_codes(): column = lax.all_gather(own, 'node', axis=0, tiled=True)  33.7 us
    ppermute x3, waiting for transfers between devices, gather_scale(): lax.ppermute(scale, 'node', [(source, (source + hop) % nodes) for source...  31.2 us
    ppermute x3, starting transfers between devices, gather_scale(): lax.ppermute(scale, 'node', [(source, (source + hop) % nodes) for source...  5.65 us
    dot_general x1, matrix products, per_device(): jnp.einsum('jrd,jdf->jrf', flat_rows, expert_in, preferred_element_type=j...  5.27 us
    dot_general x1, matrix products, per_device(): lax.dot_general(normed2, full_in, (((1,), (1,)), ((), ())), preferred_ele...  5.16 us
    dot_general x1, matrix products, per_device(): jnp.einsum('jrf,jfd->jrd', hidden, expert_out, preferred_element_type=jnp...  5.1 us
    dot_general x1, matrix products, per_device(): jnp.dot(hidden_units, full_out, preferred_element_type=jnp.float32)  3.53 us
  transfers between devices with their start and end apart: 6, of which 3 were waited for; matrix products, arithmetic and copies ran while one was open for 11% of the time, Pallas kernels for 0%

profile of v3, /device:TPU:0, one launch (start us, length us, event | category | flops | bytes accessed | tf_op | source)
XLA Modules:
  0.0 157.7 jit_solution(7860820817217492713)
XLA Ops:
  6.5 1.8 %fusion.21 = bf16[96,1536]{1,0:T(8,128)(2,1)} fusion(s32[]{:T(128)S(6)} %select_n.86, bf16[768,768]{1,0:T(8,128)(2,1)} %param.18, bf16[768,768]{1,0:T(8,128)(2,1)} %param.20), kind=kLoop, calls=%fused_computation.34 | loop fusion | flops 589824 | bytes 2654212 | tf_op jit(solution)/shard_map/concatenate | solution.py:48
  8.3 0.0 all-gather.3.cloned.1.call-update
  8.3 0.0 all-gather.5.cloned.1.call-start
  8.4 33.7 %all-gather.3.cloned.1.call-done = bf16[384,1536]{1,0:T(8,128)(2,1)} async-done(((bf16[96,1536]{1,0:T(8,128)(2,1)}), bf16[384,1536]{1,0:T(8,128)(2,1)}) %all-gather.3.cloned.1.call-update) | async-done | bytes 1179664 | tf_op jit(solution)/shard_map/all_gather | solution.py:31
  42.1 0.0 all-gather.5.cloned.1.call-update
  42.1 0.3 fusion.16
  42.4 0.2 fusion.5
  42.7 1.2 fusion.4
  43.9 0.2 copy.13
  44.1 41.5 %all_to_all.10 = bf16[2,32,16,768]{3,2,0,1:T(8,128)(2,1)S(1)} all-to-all(bf16[2,32,16,768]{3,2,0,1:T(8,128)(2,1)S(1)} %copy.13), channel_id=1, replica_groups=mesh['node'=4,'wide'=8] {'node','wide'}, dimensions={1} | all-to-all | bytes 3145728 | tf_op jit(solution)/shard_map/all_to_all | solution.py:84
  85.7 0.1 copy.14
  85.8 5.3 %maximum_convert_fusion = bf16[2,512,3072]{2,1,0:T(8,128)(2,1)S(1)} fusion(bf16[2,512,768]{2,1,0:T(8,128)(2,1)S(1)} %bitcast.16, bf16[2,768,3072]{2,1,0:T(8,128)(2,1)S(1)} %copy-done.5), kind=kOutput, calls=%fused_computation.1 | convolution fusion | flops 4838129664 | bytes 17301504 | tf_op jit(solution)/shard_map/jrd,jdf->jrf/dot_general | solution.py:86
  91.2 5.1 %convolution_convert_fusion = bf16[2,512,768]{2,1,0:T(8,128)(2,1)S(1)} fusion(bf16[2,512,3072]{2,1,0:T(8,128)(2,1)S(1)} %maximum_convert_fusion, bf16[2,3072,768]{2,1,0:T(8,128)(2,1)S(1)} %bitcast.25), kind=kOutput, calls=%fused_computation.17 | convolution fusion | flops 4832624640 | bytes 17301504 | tf_op jit(solution)/shard_map/jrf,jfd->jrd/dot_general | solution.py:88
  96.3 1.3 copy.15
  97.6 3.1 %all-to-all-start.1 = ((bf16[2,32,16,768]{3,2,0,1:T(8,128)(2,1)}), bf16[2,32,16,768]{3,2,0,1:T(8,128)(2,1)S(1)}, u32[]{:S(2)}, u32[]{:S(2)}) async-start(bf16[2,32,16,768]{3,2,0,1:T(8,128)(2,1)} %copy.15), calls=%async_computation.1 | async-start | bytes 3145728 | tf_op jit(solution)/shard_map/all_to_all | solution.py:89
  100.7 1.8 %collective-permute-start = (f32[768]{0:T(1024)S(1)}, f32[768]{0:T(1024)S(1)}, u32[]{:S(2)}, u32[]{:S(2)}) collective-permute-start(f32[768]{0:T(1024)S(1)} %copy-done.4), channel_id=1, source_target_pairs={{0,8},{8,16},{16,24},{24,0},{1,9},{9,17},{17,25},{25,1},{2,10},{10... | collective-permute-start | bytes 9224 | tf_op jit(solution)/shard_map/ppermute | solution.py:20
  102.5 2.4 %collective-permute-start.1 = (f32[768]{0:T(1024)S(1)}, f32[768]{0:T(1024)S(1)}, u32[]{:S(2)}, u32[]{:S(2)}) collective-permute-start(f32[768]{0:T(1024)S(1)} %copy-done.4), channel_id=1, source_target_pairs={{0,16},{8,24},{16,0},{24,8},{1,17},{9,25},{17,1},{25,9},{2,18},{10... | collective-permute-start | bytes 9224 | tf_op jit(solution)/shard_map/ppermute | solution.py:20
  104.9 1.4 collective-permute-start.2
  106.4 0.9 fusion.15
  107.5 0.1 dynamic_update_slice.12
  107.5 23.4 %collective-permute-done = f32[768]{0:T(1024)S(1)} collective-permute-done((f32[768]{0:T(1024)S(1)}, f32[768]{0:T(1024)S(1)}, u32[]{:S(2)}, u32[]{:S(2)}) %collective-permute-start) | collective-permute-done | bytes 3104 | tf_op jit(solution)/shard_map/ppermute | solution.py:20
  130.9 7.9 %collective-permute-done.1 = f32[768]{0:T(1024)S(1)} collective-permute-done((f32[768]{0:T(1024)S(1)}, f32[768]{0:T(1024)S(1)}, u32[]{:S(2)}, u32[]{:S(2)}) %collective-permute-start.1) | collective-permute-done | bytes 3104 | tf_op jit(solution)/shard_map/ppermute | solution.py:20
  138.9 0.2 dynamic_update_slice.15
  139.1 0.1 reshape.113
  139.2 0.1 mul.120
  139.3 0.1 copy.16
  139.5 2.0 %gather_fusion = bf16[512,768]{1,0:T(8,128)(2,1)S(1)} fusion(bf16[1024,768]{1,0:T(8,128)(2,1)S(1)} %bitcast.14, s32[1024]{0:T(1024)S(1)} %pad_clamp_fusion), kind=kCustom, calls=%fused_computation | custom fusion | bytes 1574912 | tf_op jit(solution)/shard_map/jit(_take)/gather | solution.py:96
  141.5 0.6 fusion.9
  142.1 0.0 all-gather.5.cloned.1.call-done
  142.1 0.0 copy-done.8
  142.2 5.2 %maximum_convert_fusion.1 = bf16[512,3072]{1,0:T(8,128)(2,1)S(1)} fusion(bf16[3072,1536]{1,0:T(8,128)(2,1)} %all-gather.5.cloned.1.call-done, f32[3072]{0:T(1024)S(1)} %mul.120, bf16[512,768]{1,0:T(8,128)(2,1)S(1)} %get-tuple-element.6, f32[768]{0:T(1024)S(1)} %copy-done.8, f32[512]{0:T(512)S(1)} %add_rsqrt_fusion), kind=kOutput, calls=%fused_computation.2 | convolution fusion | flops 2422210560 | bytes 8668160 | tf_op jit(solution)/shard_map/dot_general | solution.py:101
  147.4 3.5 %fusion.12 = bf16[512,768]{1,0:T(8,128)(2,1)} fusion(bf16[512,768]{1,0:T(8,128)(2,1)S(1)} %get-tuple-element.6, bf16[512,3072]{1,0:T(8,128)(2,1)S(1)} %maximum_convert_fusion.1, bf16[3072,1536]{1,0:T(8,128)(2,1)S(1)} %copy-done.6, f32[768]{0:T(1024)S(1)} %copy-done.9), kind=kOutput, calls=%fused_computation.25 | convolution fusion | flops 2417491968 | bytes 9441280 | tf_op jit(solution)/shard_map/dot_general | solution.py:105
  (44 shorter events, 0.3 us)
Async XLA Ops:
  6.5 99.9 %copy-start = (f32[768,64]{0,1:T(8,128)S(1)}, f32[768,64]{0,1:T(8,128)}, u32[]{:S(2)}) copy-start(f32[768,64]{0,1:T(8,128)} %param.14) | copy-start | bytes 589828
  6.5 35.6 %all-gather.3.cloned.1.call-start = ((), (), s32[]{:S(2)}) async-start(), calls=%async_computation.2 | async-start | bytes 1474560 | tf_op jit(solution)/shard_map/all_gather | solution.py:31
  6.5 35.6 %copy-start.3 = (s32[512,1]{0,1:T(1,128)S(1)}, s32[512,1]{0,1:T(1,128)}, u32[]{:S(2)}) copy-start(s32[512,1]{0,1:T(1,128)} %param.12) | copy-start | bytes 6148
  8.3 34.1 %copy-start.1 = (bf16[512,768]{1,0:T(8,128)(2,1)S(1)}, bf16[512,768]{1,0:T(8,128)(2,1)}, u32[]{:S(2)}) copy-start(bf16[512,768]{1,0:T(8,128)(2,1)} %param.11) | copy-start | bytes 2359300
  8.3 34.4 %copy-start.7 = (f32[768]{0:T(1024)S(1)}, f32[768]{0:T(1024)}, u32[]{:S(2)}) copy-start(f32[768]{0:T(1024)} %param.13) | copy-start | bytes 9220
  8.3 133.8 %all-gather.5.cloned.1.call-start = ((), (), s32[]{:S(2)}) async-start(), calls=%async_computation.3 | async-start | bytes 10616832 | tf_op jit(solution)/shard_map/all_gather | solution.py:32
  43.9 41.9 %copy-start.5 = (bf16[2,768,3072]{2,1,0:T(8,128)(2,1)S(1)}, bf16[2,768,3072]{2,1,0:T(8,128)(2,1)}, u32[]{:S(2)}) copy-start(bf16[2,768,3072]{2,1,0:T(8,128)(2,1)} %param.15) | copy-start | bytes 28311556
  85.7 5.4 %slice-start = ((s8[9437184]{0:T(1024)(128)(4,1)}), s8[4194304]{0:T(1024)(128)(4,1)S(1)}, s32[]{:S(2)}) async-start(s8[9437184]{0:T(1024)(128)(4,1)} %bitcast.24), calls=%async_computation.4 | async-start | bytes 8388608
  85.8 5.3 %slice-start.1 = ((s8[9437184]{0:T(1024)(128)(4,1)}), s8[4194304]{0:T(1024)(128)(4,1)S(1)}, s32[]{:S(2)}) async-start(s8[9437184]{0:T(1024)(128)(4,1)} %bitcast.24), calls=%async_computation.5 | async-start | bytes 8388608
  85.8 5.3 %slice-start.2 = ((s8[9437184]{0:T(1024)(128)(4,1)}), s8[1048576]{0:T(1024)(128)(4,1)S(1)}, s32[]{:S(2)}) async-start(s8[9437184]{0:T(1024)(128)(4,1)} %bitcast.24), calls=%async_computation.6 | async-start | bytes 2097152
  97.6 3.1 %copy-start.4 = (f32[768]{0:T(1024)S(1)}, f32[768]{0:T(1024)}, u32[]{:S(2)}) copy-start(f32[768]{0:T(1024)} %param.19) | copy-start | bytes 9220
  97.6 41.7 %all-to-all-start.1 = ((bf16[2,32,16,768]{3,2,0,1:T(8,128)(2,1)}), bf16[2,32,16,768]{3,2,0,1:T(8,128)(2,1)S(1)}, u32[]{:S(2)}, u32[]{:S(2)}) async-start(bf16[2,32,16,768]{3,2,0,1:T(8,128)(2,1)} %copy.15), calls=%async_computation.1 | async-start | bytes 3145728 | tf_op jit(solution)/shard_map/all_to_all | solution.py:89
  100.7 30.2 %collective-permute-start = (f32[768]{0:T(1024)S(1)}, f32[768]{0:T(1024)S(1)}, u32[]{:S(2)}, u32[]{:S(2)}) collective-permute-start(f32[768]{0:T(1024)S(1)} %copy-done.4), channel_id=1, source_target_pairs={{0,8},{8,16},{16,24},{24,0},{1,9},{9,17},{17,25},{25,1},{2,10},{10... | collective-permute-start | bytes 9224 | tf_op jit(solution)/shard_map/ppermute | solution.py:20
  102.5 36.3 %collective-permute-start.1 = (f32[768]{0:T(1024)S(1)}, f32[768]{0:T(1024)S(1)}, u32[]{:S(2)}, u32[]{:S(2)}) collective-permute-start(f32[768]{0:T(1024)S(1)} %copy-done.4), channel_id=1, source_target_pairs={{0,16},{8,24},{16,0},{24,8},{1,17},{9,25},{17,1},{25,9},{2,18},{10... | collective-permute-start | bytes 9224 | tf_op jit(solution)/shard_map/ppermute | solution.py:20
  104.9 34.0 %collective-permute-start.2 = (f32[768]{0:T(1024)S(1)}, f32[768]{0:T(1024)S(1)}, u32[]{:S(2)}, u32[]{:S(2)}) collective-permute-start(f32[768]{0:T(1024)S(1)} %copy-done.4), channel_id=1, source_target_pairs={{0,24},{8,0},{16,8},{24,16},{1,25},{9,1},{17,9},{25,17},{2,26},{10... | collective-permute-start | bytes 9224 | tf_op jit(solution)/shard_map/ppermute | solution.py:20
  139.4 2.1 %copy-start.2 = (bf16[512,768]{1,0:T(8,128)(2,1)S(1)}, bf16[512,768]{1,0:T(8,128)(2,1)}, u32[]{:S(2)}) copy-start(bf16[512,768]{1,0:T(8,128)(2,1)} %param.11) | copy-start | bytes 2359300
  141.5 0.7 copy-start.8
  142.2 5.2 %copy-start.6 = (bf16[3072,1536]{1,0:T(8,128)(2,1)S(1)}, bf16[3072,1536]{1,0:T(8,128)(2,1)}, u32[]{:S(2)}) copy-start(bf16[3072,1536]{1,0:T(8,128)(2,1)} %all-gather.5.cloned.1.call-done) | copy-start | bytes 28311556
  142.2 5.2 %copy-start.9 = (f32[768]{0:T(1024)S(1)}, f32[768]{0:T(1024)}, u32[]{:S(2)}) copy-start(f32[768]{0:T(1024)} %param.21) | copy-start | bytes 9220
Sparse Core Ops, SparseCore 0:
  8.9 33.1 all-gather.2
  44.0 83.9 all-gather.4
